TPU v7x, 32 devices: a whole 2x2x4 slice. The times are simulated.
32 devices in a mesh: req: 8 (over z, x), tp: 4 (over y, core).
Axes of the slice: x: 2, y: 2, z: 4, core: 2. Of those that a mesh axis runs over, the one named last changes fastest.
Arguments:
- queries: bfloat16 [1024, 3584], P('req', 'tp'), may hold values from -13 to 13
- tree_kv: bfloat16 [1024, 4, 256], P('req', 'tp'), may hold values from -5 to 5
- page_pool: bfloat16 [96, 4, 128, 256], P('req', 'tp'), may hold values from -5 to 5
- page_table: int32 [16, 8], P('req'), may hold values from 0 to 11, as said below
- cache_len: int32 [16], P('req'), may hold values from 1 to 1024
- parents: int32 [16, 64], P('req'), may hold values from -1 to 62, as said below
- accepted: int32 [16], P('req'), may hold values from 0 to 63
- o_weight: bfloat16 [3584, 1792], P('tp'), may hold values from -0.5 to 0.5
Outputs:
- projected: bfloat16 [1024, 1792], P(('req', 'tp'))
- kept_rows: bfloat16 [1024, 4, 256], P('req', 'tp')
Inputs may be any that keep to these rules, and one draw needn't show every extreme that they name: Logical page k of request r is in slot page_table[r, k] of its own device's pool for k < 2, among that pool's first 4 slots, and for k >= 2 in that slot of the next req device's pool (the first device after the last), among its last 8 slots; distinct pages are in distinct slots; entries at k >= ceil(cache_len[r] / 128) are 0. parents[r, 0] = -1 and 0 <= parents[r, j] < j for j >= 1.
All inputs are finite; a program needn't handle non-finite values.
Results may differ from a plain program's by a relative error of at most 0.007.
Values may be sent and summed in bfloat16 or wider, within the bound.
A program may use at most 64 MiB of HBM per device.

v0:
```python
import math

import jax
import jax.numpy as jnp
from jax import lax
from jax.sharding import PartitionSpec as P

HEAD_SIZE = 128
LOCAL = 2


very_negative = -1e30


def from_behind(block, axis, distance):
    devices = range(lax.axis_size(axis))
    route = [((i - distance) % len(devices), i) for i in devices]
    return lax.ppermute(block, axis, route)


def ancestors(parent_row):
    tree_len = parent_row.shape[0]
    node_ids = jnp.arange(tree_len, dtype=jnp.int32)
    parent_links = (parent_row[:, None] == node_ids[None, :]).astype(jnp.float32)
    reachable = jnp.eye(tree_len, dtype=jnp.float32) + parent_links
    for squaring in range((tree_len - 1).bit_length()):
        reachable = jnp.minimum(jnp.dot(reachable, reachable, precision=lax.Precision.HIGHEST), 1.0)
    return reachable


def block_stats(query_rows, block_keys, block_values, visible):
    scores = jnp.einsum(
        "tgd,nd->tgn", query_rows, block_keys, preferred_element_type=jnp.float32
    ) * (1.0 / math.sqrt(query_rows.shape[-1]))
    scores = jnp.where(visible, scores, very_negative)
    maxima = jnp.max(scores, axis=-1)
    weights = jnp.where(visible, jnp.exp(scores - maxima[..., None]), 0.0).astype(jnp.bfloat16)
    totals = jnp.sum(weights.astype(jnp.float32), axis=-1)
    accums = jnp.einsum("tgn,nd->tgd", weights, block_values, preferred_element_type=jnp.float32)
    return (maxima, totals, accums)


def combine(first_state, second_state):
    joined_max = jnp.maximum(first_state[0], second_state[0])
    first_factor = jnp.exp(first_state[0] - joined_max)
    second_factor = jnp.exp(second_state[0] - joined_max)
    totals = first_factor * first_state[1] + second_factor * second_state[1]
    accums = first_factor[..., None] * first_state[2] + second_factor[..., None] * second_state[2]
    return (joined_max, totals, accums)


def pages_partial(query_rows, pages, visible):
    head_dim = query_rows.shape[-1]
    scores = jnp.einsum(
        "tgd,knd->tgkn", query_rows, pages[..., :head_dim], preferred_element_type=jnp.float32
    ) * (1.0 / math.sqrt(head_dim))
    mask = visible[None, None, :, :]
    scores = jnp.where(mask, scores, very_negative)
    maxima = jnp.max(scores, axis=-1)
    weights = jnp.where(mask, jnp.exp(scores - maxima[..., None]), 0.0).astype(jnp.bfloat16)
    totals = jnp.sum(weights.astype(jnp.float32), axis=-1)
    accums = jnp.einsum(
        "tgkn,knd->tgkd", weights, pages[..., head_dim:], preferred_element_type=jnp.float32
    )
    overall = jnp.max(maxima, axis=-1)
    factors = jnp.exp(maxima - overall[..., None])
    total = jnp.sum(factors * totals, axis=-1)
    accum = jnp.sum(factors[..., None] * accums, axis=2)
    return (overall, total, accum)


def sweep_all(query_rows, pool_slots, tables, lengths, first_page):
    page_len = pool_slots.shape[1]
    page_count = tables.shape[1]
    offsets = jnp.arange(page_len, dtype=jnp.int32)
    page_numbers = first_page + jnp.arange(page_count, dtype=jnp.int32)
    positions = page_numbers[:, None] * page_len + offsets[None, :]

    def one_request(request_data):
        request_query, table_row, length = request_data
        pages = jnp.take(pool_slots, table_row, axis=0)
        visible = positions < length
        return pages_partial(request_query, pages, visible)

    return lax.map(one_request, (query_rows, tables, lengths))


def shards(queries, tree_kv, page_pool, page_table, cache_len, parents, accepted, o_weight):
    requests = page_table.shape[0]
    tree_len = parents.shape[1]
    group_size = queries.shape[1] // HEAD_SIZE
    query_rows = queries.reshape(requests, tree_len, group_size, HEAD_SIZE)
    tree_rows = tree_kv[:, 0, :].reshape(requests, tree_len, 2 * HEAD_SIZE)
    pool_slots = page_pool[:, 0]
    reachable = jax.vmap(ancestors)(parents)
    page_meta = jnp.concatenate([page_table, cache_len[:, None]], axis=1)
    moved_queries, moved_meta = from_behind((queries, page_meta), "req", 1)
    moved_rows = moved_queries.reshape(requests, tree_len, group_size, HEAD_SIZE)
    partial_value = sweep_all(
        moved_rows, pool_slots, moved_meta[:, LOCAL:-1], moved_meta[:, -1], LOCAL
    )
    returned = from_behind((partial_value[2], partial_value[0], partial_value[1]), "req", -1)
    local_state = sweep_all(query_rows, pool_slots, page_table[:, :LOCAL], cache_len, 0)
    page_state = combine(local_state, (returned[1], returned[2], returned[0]))
    tree_visible = (reachable > 0.5)[:, :, None, :]
    tree_state = jax.vmap(block_stats)(
        query_rows, tree_rows[:, :, :HEAD_SIZE], tree_rows[:, :, HEAD_SIZE:], tree_visible
    )
    merged = combine(page_state, tree_state)
    attention = (
        (merged[2] / merged[1][..., None])
        .astype(jnp.bfloat16)
        .reshape(requests * tree_len, group_size * HEAD_SIZE)
    )
    rows_out = attention.shape[0] // lax.axis_size("tp")
    whole_sum = lax.psum(jnp.dot(attention, o_weight, preferred_element_type=jnp.float32), "tp")
    summed = lax.dynamic_slice_in_dim(whole_sum, lax.axis_index("tp") * rows_out, rows_out, 0)
    projected = summed.astype(jnp.bfloat16)
    node_ids = jnp.arange(tree_len, dtype=jnp.int32)
    leaf_onehot = (accepted[:, None] == node_ids[None, :]).astype(jnp.float32)
    kept_mask = jnp.einsum("rm,rmn->rn", leaf_onehot, reachable, precision=lax.Precision.HIGHEST)
    depths = jnp.sum(reachable, axis=2) - 1.0
    slot_ids = jnp.arange(tree_len, dtype=jnp.float32)
    selector = (
        kept_mask[:, None, :] * (depths[:, None, :] == slot_ids[None, :, None]).astype(jnp.float32)
    ).astype(jnp.bfloat16)
    kept = jnp.einsum(
        "rsm,rmc->rsc", selector, tree_rows, preferred_element_type=jnp.float32
    ).astype(jnp.bfloat16)
    return (projected, kept.reshape(requests * tree_len, 1, 2 * HEAD_SIZE))


def solution(mesh):
    in_specs = (
        P("req", "tp"),
        P("req", "tp", None),
        P("req", "tp", None, None),
        P("req", None),
        P("req"),
        P("req", None),
        P("req"),
        P("tp", None),
    )
    out_specs = (P(("req", "tp"), None), P("req", "tp", None))
    return jax.shard_map(shards, mesh=mesh, in_specs=in_specs, out_specs=out_specs, check_vma=False)
```

profile of v0, /device:TPU:27, one launch (start us, length us, event | category | flops | bytes accessed | tf_op | source)
XLA Modules:
  0.0 108.4 jit_solution(3384469890110237397)
XLA Ops:
  1.5 1.4 %pad_add_fusion = s32[2,9]{1,0:T(2,128)} fusion(s32[2,1]{1,0:T(2,128)S(1)} %copy.48, s32[2,8]{1,0:T(2,128)} %param.15), kind=kLoop, calls=%fused_computation.98 | loop fusion | flops 18 | bytes 144 | tf_op jit(solution)/shard_map/concatenate | solution.py:96
  5.8 1.3 %compare_bitcast_fusion = pred[2,64,1]{1,0,2:T(4,128)(4,1)} fusion(s32[2]{0:T(128)} %param.18), kind=kLoop, calls=%fused_computation.97 | loop fusion | flops 128 | bytes 136 | tf_op jit(solution)/shard_map/eq | solution.py:120
  11.3 1.4 %fusion.35 = f32[2,1,64]{2,1,0:T(1,128)} fusion(f32[2,64,64]{2,1,0:T(8,128)S(1)} %get-tuple-element.262, pred[2,64,1]{1,0,2:T(4,128)(4,1)} %compare_bitcast_fusion), kind=kOutput, calls=%fused_computation.95 | convolution fusion | flops 98304 | bytes 33408 | tf_op jit(solution)/shard_map/rm,rmn->rn/dot_general | solution.py:121
  14.2 17.2 %while.30 = (s32[]{:T(128)}, f32[2,64,7]{1,2,0:T(8,128)S(1)}, f32[2,64,7]{1,2,0:T(8,128)S(1)}, f32[2,64,7,128]{3,1,2,0:T(8,128)}, s32[2]{0:T(128)}, /*index=5*/b...) while((s32[]{:T(128)}, f32[2,64,7]{1,2,0:T(8,128)S(1)}, ...), condition=%wide.region_6.7_spmd.clone, body=%wide.region_0.6_spmd.clone.sunk | while | flops 59991572 | bytes 6568445 | solution.py:85
  14.2 1.3 %dynamic_slice.66 = s32[1]{0:T(128)} dynamic-slice(s32[2]{0:T(128)} %get-tuple-element.465, s32[]{:T(128)S(6)} %copy.108), dynamic_slice_sizes={1} | dynamic-slice | bytes 12 | tf_op jit(solution)/shard_map/while/body/jit(dynamic_index_in_dim)/dynamic_slice | solution.py:85
  15.5 1.3 %add_compare_fusion.4 = pred[2,128]{1,0:T(4,128)(4,1)S(1)} fusion(s32[2]{0:T(128)} %get-tuple-element.469, s32[]{:T(128)} %bitcast.143), kind=kLoop, calls=%fused_computation.28.clone.1 | loop fusion | flops 512 | bytes 268 | tf_op jit(solution)/shard_map/while/body/eval_jaxpr/lt | solution.py:82
  18.2 1.7 %gather_fusion = bf16[2,128,256]{2,1,0:T(8,128)(2,1)S(1)} fusion(bf16[12,128,256]{2,1,0:T(8,128)(2,1)} %get-tuple-element.468, s32[1024]{0:T(1024)S(1)} %pad_clamp_fusion.4), kind=kCustom, calls=%fused_computation.clone.clone.1 | custom fusion | bytes 262152 | tf_op jit(solution)/shard_map/while/body/eval_jaxpr/jit(_take)/gather | solution.py:81
  20.0 1.4 %fusion.68 = (f32[64,7,2]{0,2,1:T(2,128)S(1)}, f32[64,7]{0,1:T(8,128)S(1)}, f32[64,7,2,128]{3,0,2,1:T(8,128)S(1)}) fusion(bf16[2,128,256]{2,1,0:T(8,128)(2,1)S(1)} %broadcast_select_fusion.4, bf16[2,64,7,128]{3,1,2,0:T(8,128)(2,1)} %get-tuple-element.466, s32[]{:T(128)S(6)} %copy.108, pred[2,128]{1,0:T(4,128)(4,1)S(1)} %add_compare_fusion.4), kind=kOutput, calls=%fused_computation.105.clone.1 | convolution fusion | flops 29817536 | bytes 644868 | tf_op jit(solution)/shard_map/while/body/eval_jaxpr/tgd,knd->tgkn/dot_general | solution.py:54
  22.8 1.2 %dynamic_slice.66 = s32[1]{0:T(128)} dynamic-slice(s32[2]{0:T(128)} %get-tuple-element.465, s32[]{:T(128)S(6)} %copy.108), dynamic_slice_sizes={1} | dynamic-slice | bytes 12 | tf_op jit(solution)/shard_map/while/body/jit(dynamic_index_in_dim)/dynamic_slice | solution.py:85
  24.1 1.3 %add_compare_fusion.4 = pred[2,128]{1,0:T(4,128)(4,1)S(1)} fusion(s32[2]{0:T(128)} %get-tuple-element.469, s32[]{:T(128)} %bitcast.143), kind=kLoop, calls=%fused_computation.28.clone.1 | loop fusion | flops 512 | bytes 268 | tf_op jit(solution)/shard_map/while/body/eval_jaxpr/lt | solution.py:82
  26.8 1.7 %gather_fusion = bf16[2,128,256]{2,1,0:T(8,128)(2,1)S(1)} fusion(bf16[12,128,256]{2,1,0:T(8,128)(2,1)} %get-tuple-element.468, s32[1024]{0:T(1024)S(1)} %pad_clamp_fusion.4), kind=kCustom, calls=%fused_computation.clone.clone.1 | custom fusion | bytes 262152 | tf_op jit(solution)/shard_map/while/body/eval_jaxpr/jit(_take)/gather | solution.py:81
  28.6 1.4 %fusion.68 = (f32[64,7,2]{0,2,1:T(2,128)S(1)}, f32[64,7]{0,1:T(8,128)S(1)}, f32[64,7,2,128]{3,0,2,1:T(8,128)S(1)}) fusion(bf16[2,128,256]{2,1,0:T(8,128)(2,1)S(1)} %broadcast_select_fusion.4, bf16[2,64,7,128]{3,1,2,0:T(8,128)(2,1)} %get-tuple-element.466, s32[]{:T(128)S(6)} %copy.108, pred[2,128]{1,0:T(4,128)(4,1)S(1)} %add_compare_fusion.4), kind=kOutput, calls=%fused_computation.105.clone.1 | convolution fusion | flops 29817536 | bytes 644868 | tf_op jit(solution)/shard_map/while/body/eval_jaxpr/tgd,knd->tgkn/dot_general | solution.py:54
  31.4 1.3 %fusion.43 = (f32[2,64,7]{1,2,0:T(8,128)S(1)}, f32[2,64,7,64]{1,3,2,0:T(8,128)S(1)}) fusion(bf16[2,64,7,128]{3,1,2,0:T(8,128)(2,1)} %get-tuple-element.472, bf16[2,64,256]{2,1,0:T(8,128)(2,1)S(1)} %bitcast.156, pred[2,64,64]{1,2,0:T(8,128)(4,1)S(1)} %copy.52), kind=kOutput, calls=%fused_computation.107 | convolution fusion | flops 14851200 | bytes 511488 | tf_op jit(solution)/shard_map/vmap(tgd,nd->tgn)/dot_general | solution.py:32
  35.7 1.3 %slice.29 = s32[2,6]{1,0:T(2,128)} slice(s32[2,9]{1,0:T(2,128)} %collective-permute-done), slice={[0:2], [2:8]} | slice | bytes 96 | tf_op jit(solution)/shard_map/slice | solution.py:100
  37.0 1.4 %slice_reduce_fusion = s32[2]{0:T(128)} fusion(s32[2,9]{1,0:T(2,128)} %collective-permute-done), kind=kLoop, calls=%fused_computation.99 | loop fusion | bytes 16 | tf_op jit(solution)/shard_map/slice | solution.py:100
  38.4 1.2 %reshape.135 = bf16[2,64,7,128]{3,2,1,0:T(8,128)(2,1)S(1)} reshape(bf16[128,896]{1,0:T(8,128)(2,1)} %collective-permute-done.1) | data formatting | bytes 458752 | tf_op jit(solution)/shard_map/reshape | solution.py:98
  42.4 23.4 %while.31 = (s32[]{:T(128)}, f32[2,64,7]{1,2,0:T(8,128)}, f32[2,64,7]{1,2,0:T(8,128)}, f32[2,64,7,128]{3,1,2,0:T(8,128)}, s32[2]{0:T(128)}, /*index=5*/bf16[2,64...) while((s32[]{:T(128)}, f32[2,64,7]{1,2,0:T(8,128)}, ...), condition=%wide.region_13.14_spmd.clone, body=%wide.region_7.13_spmd.clone.sunk | while | flops 180089152 | bytes 11682033 | solution.py:85
  42.4 1.3 %dynamic_slice.70 = s32[1]{0:T(128)} dynamic-slice(s32[2]{0:T(128)} %get-tuple-element.435, s32[]{:T(128)S(6)} %copy.96), dynamic_slice_sizes={1} | dynamic-slice | bytes 12 | tf_op jit(solution)/shard_map/while/body/jit(dynamic_index_in_dim)/dynamic_slice | solution.py:85
  43.7 1.4 %add_compare_fusion.5 = pred[6,128]{1,0:T(8,128)(4,1)S(1)} fusion(s32[6]{0:T(128)} %get-tuple-element.439, s32[]{:T(128)} %bitcast.153), kind=kLoop, calls=%fused_computation.49.clone.1 | loop fusion | flops 1536 | bytes 796 | tf_op jit(solution)/shard_map/while/body/eval_jaxpr/lt | solution.py:82
  45.8 1.3 %compare_and_fusion.5 = pred[6]{0:T(512)(128)(4,1)} fusion(s32[2,6]{1,0:T(2,128)} %get-tuple-element.437, s32[]{:T(128)S(6)} %copy.96), kind=kLoop, calls=%fused_computation.52.clone.1 | loop fusion | flops 36 | bytes 34 | tf_op jit(solution)/shard_map/while/body/eval_jaxpr/jit(_take)/and | solution.py:81
  47.1 2.5 %gather_fusion.1 = bf16[6,128,256]{2,1,0:T(8,128)(2,1)} fusion(bf16[12,128,256]{2,1,0:T(8,128)(2,1)} %get-tuple-element.438, s32[1024]{0:T(1024)S(1)} %pad_clamp_fusion.5), kind=kCustom, calls=%fused_computation.1.clone.clone.1 | custom fusion | bytes 786456 | tf_op jit(solution)/shard_map/while/body/eval_jaxpr/jit(_take)/gather | solution.py:81
  54.1 1.3 %dynamic_slice.70 = s32[1]{0:T(128)} dynamic-slice(s32[2]{0:T(128)} %get-tuple-element.435, s32[]{:T(128)S(6)} %copy.96), dynamic_slice_sizes={1} | dynamic-slice | bytes 12 | tf_op jit(solution)/shard_map/while/body/jit(dynamic_index_in_dim)/dynamic_slice | solution.py:85
  55.4 1.4 %add_compare_fusion.5 = pred[6,128]{1,0:T(8,128)(4,1)S(1)} fusion(s32[6]{0:T(128)} %get-tuple-element.439, s32[]{:T(128)} %bitcast.153), kind=kLoop, calls=%fused_computation.49.clone.1 | loop fusion | flops 1536 | bytes 796 | tf_op jit(solution)/shard_map/while/body/eval_jaxpr/lt | solution.py:82
  57.5 1.3 %compare_and_fusion.5 = pred[6]{0:T(512)(128)(4,1)} fusion(s32[2,6]{1,0:T(2,128)} %get-tuple-element.437, s32[]{:T(128)S(6)} %copy.96), kind=kLoop, calls=%fused_computation.52.clone.1 | loop fusion | flops 36 | bytes 34 | tf_op jit(solution)/shard_map/while/body/eval_jaxpr/jit(_take)/and | solution.py:81
  58.8 2.5 %gather_fusion.1 = bf16[6,128,256]{2,1,0:T(8,128)(2,1)} fusion(bf16[12,128,256]{2,1,0:T(8,128)(2,1)} %get-tuple-element.438, s32[1024]{0:T(1024)S(1)} %pad_clamp_fusion.5), kind=kCustom, calls=%fused_computation.1.clone.clone.1 | custom fusion | bytes 786456 | tf_op jit(solution)/shard_map/while/body/eval_jaxpr/jit(_take)/gather | solution.py:81
  66.1 1.4 %convolution_convert_fusion = bf16[2,64,256]{2,1,0:T(8,128)(2,1)} fusion(bf16[2,64,256]{2,1,0:T(8,128)(2,1)S(1)} %bitcast.158, f32[2,64]{1,0:T(2,128)} %bitcast.160, f32[2,64]{1,0:T(2,128)} %broadcast_add_fusion), kind=kOutput, calls=%fused_computation.58 | convolution fusion | flops 4243456 | bytes 132096 | tf_op jit(solution)/shard_map/rsm,rmc->rsc/dot_general | solution.py:127
  67.6 2.3 %collective-permute-start.2 = (f32[2,64,7]{1,2,0:T(8,128)}, f32[2,64,7]{1,2,0:T(8,128)S(1)}, u32[]{:S(2)}, u32[]{:S(2)}) collective-permute-start(f32[2,64,7]{1,2,0:T(8,128)} %get-tuple-element.101), channel_id=1, source_target_pairs={{4,0},{8,4},{12,8},{16,12},{20,16},{24,20},{28,24},{0,28},{5,1},{9... | collective-permute-start | bytes 10760 | tf_op jit(solution)/shard_map/ppermute | solution.py:18
  71.3 8.4 %collective-permute-done.2 = f32[2,64,7]{1,2,0:T(8,128)S(1)} collective-permute-done((f32[2,64,7]{1,2,0:T(8,128)}, f32[2,64,7]{1,2,0:T(8,128)S(1)}, u32[]{:S(2)}, u32[]{:S(2)}) %collective-permute-start.2) | collective-permute-done | bytes 3616 | tf_op jit(solution)/shard_map/ppermute | solution.py:18
  79.9 1.9 %divide_convert_fusion = bf16[2,64,7,128]{3,1,2,0:T(8,128)(2,1)S(1)} fusion(f32[2,64,7,128]{3,1,2,0:T(8,128)} %fusion.26, f32[2,64,7,128]{3,1,2,0:T(8,128)} %collective-permute-done.3, f32[2,64,7,128]{3,1,2,0:T(8,128)} %get-tuple-element.102, f32[2,64,7]{1,2,0:T(8,128)S(1)} %get-tuple-element.250, f32[2,64,7]{1,2,0:T(8,128)S(1)} %get-tuple-element.254, ...), kind=kLoop, calls=%fused_computation.65 | loop fusion | flops 917504 | bytes 1623552 | tf_op jit(solution)/shard_map/convert_element_type | solution.py:112
  82.0 1.6 %fusion.21 = f32[128,1792]{1,0:T(8,128)} fusion(bf16[896,1792]{1,0:T(8,128)(2,1)S(1)} %copy-done, bf16[16,8,7,128]{3,2,1,0:T(8,128)(2,1)S(1)} %bitcast.155), kind=kOutput, calls=%fused_computation.68 | convolution fusion | flops 411041792 | bytes 4358144 | tf_op jit(solution)/shard_map/dot_general | solution.py:116
  83.6 23.2 %all-reduce.1 = bf16[128,1792]{1,0:T(8,128)(2,1)} all-reduce(f32[128,1792]{1,0:T(8,128)} %fusion.21), channel_id=1, replica_groups=mesh['req'=8,'tp'=4] {'tp'}, use_global_device_ids=true, to_apply=%region_16.17 | all-reduce | flops 229376 | bytes 1376256 | tf_op jit(solution)/shard_map/psum | solution.py:116
  106.9 1.6 %dynamic-slice_convert_fusion = bf16[32,1792]{1,0:T(8,128)(2,1)} fusion(bf16[128,1792]{1,0:T(8,128)(2,1)} %all-reduce.1, s32[]{:T(128)S(6)} %select_n.66), kind=kLoop, calls=%fused_computation.71 | loop fusion | bytes 229380 | tf_op jit(solution)/shard_map/convert_element_type | solution.py:118
  (130 shorter events, 33.2 us)
Async XLA Ops:
  0.6 81.4 %copy-start = (bf16[896,1792]{1,0:T(8,128)(2,1)S(1)}, bf16[896,1792]{1,0:T(8,128)(2,1)}, u32[]{:S(2)}) copy-start(bf16[896,1792]{1,0:T(8,128)(2,1)} %param.19) | copy-start | bytes 9633796
  2.9 32.8 %collective-permute-start = (s32[2,9]{1,0:T(2,128)}, s32[2,9]{1,0:T(2,128)}, u32[]{:S(2)}, u32[]{:S(2)}) collective-permute-start(s32[2,9]{1,0:T(2,128)} %pad_add_fusion), channel_id=1, source_target_pairs={{28,0},{0,4},{4,8},{8,12},{12,16},{16,20},{20,24},{24,28},{29,1},{... | collective-permute-start | bytes 224 | tf_op jit(solution)/shard_map/ppermute | solution.py:18
  2.9 35.5 %collective-permute-start.1 = (bf16[128,896]{1,0:T(8,128)(2,1)}, bf16[128,896]{1,0:T(8,128)(2,1)}, u32[]{:S(2)}, u32[]{:S(2)}) collective-permute-start(bf16[128,896]{1,0:T(8,128)(2,1)} %param.12), channel_id=1, source_target_pairs={{28,0},{0,4},{4,8},{8,12},{12,16},{16,20},{20,24},{24,28},{29,1},{... | collective-permute-start | bytes 688136 | tf_op jit(solution)/shard_map/ppermute | solution.py:18
  14.2 17.2 %copy-start.6 = (bf16[128,1,256]{2,0,1:T(8,128)(2,1)S(1)}, bf16[128,1,256]{2,0,1:T(8,128)(2,1)}, u32[]{:S(2)}) copy-start(bf16[128,1,256]{2,0,1:T(8,128)(2,1)} %param.13) | copy-start | bytes 196612
  19.9 2.1 %copy-start.2 = (f32[2,64,7,128]{3,1,2,0:T(8,128)S(1)}, f32[2,64,7,128]{3,1,2,0:T(8,128)}, u32[]{:S(2)}) copy-start(f32[2,64,7,128]{3,1,2,0:T(8,128)} %get-tuple-element.454) | copy-start | bytes 1376260 | tf_op jit(solution)/shard_map/while
  22.1 0.8 copy-start.3
  28.5 2.1 %copy-start.2 = (f32[2,64,7,128]{3,1,2,0:T(8,128)S(1)}, f32[2,64,7,128]{3,1,2,0:T(8,128)}, u32[]{:S(2)}) copy-start(f32[2,64,7,128]{3,1,2,0:T(8,128)} %get-tuple-element.454) | copy-start | bytes 1376260 | tf_op jit(solution)/shard_map/while
  31.4 7.0 %copy-start.10 = (f32[2,64,7]{1,2,0:T(8,128)}, f32[2,64,7]{1,2,0:T(8,128)S(1)}, u32[]{:S(2)}) copy-start(f32[2,64,7]{1,2,0:T(8,128)S(1)} %get-tuple-element.100) | copy-start | bytes 10756
  31.4 7.0 %copy-start.12 = (f32[2,64,7]{1,2,0:T(8,128)}, f32[2,64,7]{1,2,0:T(8,128)S(1)}, u32[]{:S(2)}) copy-start(f32[2,64,7]{1,2,0:T(8,128)S(1)} %get-tuple-element.104) | copy-start | bytes 10756
  31.4 3.1 %copy-start.18 = (f32[2,64]{1,0:T(2,128)S(1)}, f32[2,64]{1,0:T(2,128)}, u32[]{:S(2)}) copy-start(f32[2,64]{1,0:T(2,128)} %reduce_sum.73) | copy-start | bytes 1540
  32.7 0.8 copy-start.1
  32.7 1.8 %copy-start.8 = (f32[2,64,7]{1,2,0:T(8,128)}, f32[2,64,7]{1,2,0:T(8,128)S(1)}, u32[]{:S(2)}) copy-start(f32[2,64,7]{1,2,0:T(8,128)S(1)} %get-tuple-element.263) | copy-start | bytes 10756
  42.4 27.8 %copy-start.9 = (f32[2,64,7]{1,2,0:T(8,128)S(1)}, f32[2,64,7]{1,2,0:T(8,128)}, u32[]{:S(2)}) copy-start(f32[2,64,7]{1,2,0:T(8,128)} %copy-done.8) | copy-start | bytes 10756
  42.4 37.5 %copy-start.11 = (f32[2,64,7]{1,2,0:T(8,128)S(1)}, f32[2,64,7]{1,2,0:T(8,128)}, u32[]{:S(2)}) copy-start(f32[2,64,7]{1,2,0:T(8,128)} %copy-done.10) | copy-start | bytes 10756
  42.4 37.5 %copy-start.13 = (f32[2,64,7]{1,2,0:T(8,128)S(1)}, f32[2,64,7]{1,2,0:T(8,128)}, u32[]{:S(2)}) copy-start(f32[2,64,7]{1,2,0:T(8,128)} %copy-done.12) | copy-start | bytes 10756
  42.4 8.3 %copy-start.7 = (bf16[2,64,7,128]{3,1,2,0:T(8,128)(2,1)S(1)}, bf16[2,64,7,128]{3,1,2,0:T(8,128)(2,1)}, u32[]{:S(2)}) copy-start(bf16[2,64,7,128]{3,1,2,0:T(8,128)(2,1)} %get-tuple-element.436) | copy-start | bytes 688132 | tf_op jit(solution)/shard_map/while
  51.4 0.9 copy-start.14
  51.4 0.9 copy-start.16
  52.2 1.0 copy-start.4
  52.3 1.0 copy-start.15
  52.3 1.0 copy-start.17
  53.3 0.8 copy-start.5
  54.1 8.3 %copy-start.7 = (bf16[2,64,7,128]{3,1,2,0:T(8,128)(2,1)S(1)}, bf16[2,64,7,128]{3,1,2,0:T(8,128)(2,1)}, u32[]{:S(2)}) copy-start(bf16[2,64,7,128]{3,1,2,0:T(8,128)(2,1)} %get-tuple-element.436) | copy-start | bytes 688132 | tf_op jit(solution)/shard_map/while
  63.1 0.9 copy-start.14
  63.1 0.9 copy-start.16
  63.9 1.0 copy-start.4
  64.0 1.0 copy-start.15
  64.0 1.0 copy-start.17
  65.0 0.8 copy-start.5
  65.7 14.2 %collective-permute-start.3 = (f32[2,64,7,128]{3,1,2,0:T(8,128)}, f32[2,64,7,128]{3,1,2,0:T(8,128)}, u32[]{:S(2)}, u32[]{:S(2)}) collective-permute-start(f32[2,64,7,128]{3,1,2,0:T(8,128)} %get-tuple-element.103), channel_id=1, source_target_pairs={{4,0},{8,4},{12,8},{16,12},{20,16},{24,20},{28,24},{0,28},{5,1},{9... | collective-permute-start | bytes 1376264 | tf_op jit(solution)/shard_map/ppermute | solution.py:18
  67.6 12.2 %collective-permute-start.2 = (f32[2,64,7]{1,2,0:T(8,128)}, f32[2,64,7]{1,2,0:T(8,128)S(1)}, u32[]{:S(2)}, u32[]{:S(2)}) collective-permute-start(f32[2,64,7]{1,2,0:T(8,128)} %get-tuple-element.101), channel_id=1, source_target_pairs={{4,0},{8,4},{12,8},{16,12},{20,16},{24,20},{28,24},{0,28},{5,1},{9... | collective-permute-start | bytes 10760 | tf_op jit(solution)/shard_map/ppermute | solution.py:18
  69.9 10.0 %collective-permute-start.4 = (f32[2,64,7]{1,2,0:T(8,128)}, f32[2,64,7]{1,2,0:T(8,128)S(1)}, u32[]{:S(2)}, u32[]{:S(2)}) collective-permute-start(f32[2,64,7]{1,2,0:T(8,128)} %get-tuple-element.105), channel_id=1, source_target_pairs={{4,0},{8,4},{12,8},{16,12},{20,16},{24,20},{28,24},{0,28},{5,1},{9... | collective-permute-start | bytes 10760 | tf_op jit(solution)/shard_map/ppermute | solution.py:18
  (1 other events, 0.8 us)
where the time goes:
time: 110 us; the launch traced here: 108 us
  local copies, waits for them, and re-layouts  31.3 us (28%)
  other arithmetic  25.1 us (23%)
  blocking collectives  23.2 us (21%)
  matrix products  14.8 us (13%)
  waiting for transfers between devices  8.62 us (8%)
  starting transfers between devices  4.08 us (4%)
    psum x1, blocking collectives, shards(): lax.psum(jnp.dot(attention, o_weight, preferred_element_type=jnp.float32)...  23.2 us
    ppermute x5, waiting for transfers between devices, from_behind(): return lax.ppermute(block, axis, route)  8.62 us
    gather x4, local copies, waits for them, and re-layouts, one_request(): pages = jnp.take(pool_slots, table_row, axis=0)  8.31 us
    lt x4, other arithmetic, one_request(): visible = positions < length  5.47 us
    dynamic_slice x4, local copies, waits for them, and re-layouts, sweep_all(): return lax.map(one_request, (query_rows, tables, lengths))  5.16 us
    select_n x8, other arithmetic, one_request(): pages = jnp.take(pool_slots, table_row, axis=0)  5.11 us
    dot_general x4, matrix products, pages_partial(): jnp.einsum('tgd,knd->tgkn', query_rows, pages[..., :head_dim], preferred_...  4.11 us
    ppermute x5, starting transfers between devices, from_behind(): return lax.ppermute(block, axis, route)  4.08 us
  transfers between devices with their start and end apart: 5, of which 2 were waited for; matrix products, arithmetic and copies ran while one was open for 32% of the time, Pallas kernels for 0%

commit v1 on v0

v1 whole, which is shorter than its diff:
```python
import functools
import math

import jax
import jax.numpy as jnp
from jax import lax
from jax.experimental import pallas as pl
from jax.experimental.pallas import tpu as pltpu
from jax.sharding import PartitionSpec as P

HEAD_SIZE = 128
LOCAL = 2
COLS = 256
K_PIECES = 2
V_PIECES = 4

very_negative = -1e30
MESH = pl.DeviceIdType.MESH
f32 = jnp.float32
bf16 = jnp.bfloat16


def dot_t(a, b):
    return lax.dot_general(a, b, (((1,), (1,)), ((), ())), preferred_element_type=f32)


def kernel(
    table_ref,
    len_ref,
    acc_ref,
    parents_ref,
    q_hbm,
    tree_hbm,
    pool_hbm,
    w_hbm,
    out_ref,
    kept_ref,
    q_ref,
    tree_ref,
    own_ref,
    w_ref,
    k_ref,
    v_ref,
    s_ref,
    p_ref,
    sum_ref,
    att_ref,
    part_ref,
    send1,
    recv1,
    send2,
    recv2,
    load_sems,
    ks_sems,
    kr_sems,
    vs_sems,
    vr_sems,
    s1_sems,
    r1_sems,
    s2_sems,
    r2_sems,
):
    requests, max_pages = table_ref.shape
    tree = parents_ref.shape[1]
    tokens = requests * tree
    page = pool_hbm.shape[1]
    spill = k_ref.shape[0]
    own = own_ref.shape[0]
    group = q_ref.shape[1] // HEAD_SIZE
    rows = group * tree
    chunks = part_ref.shape[0]
    tp_size = part_ref.shape[1]
    scale = 1.0 / math.sqrt(HEAD_SIZE)

    n = lax.axis_size("req")
    me = lax.axis_index("req")
    before, after = lax.rem(me + n - 1, n), lax.rem(me + 1, n)
    tp = lax.axis_index("tp")
    low, high = lax.rem(tp, 2), tp // 2
    mate1 = high * 2 + (1 - low)
    mate2 = (1 - high) * 2 + low

    loads = [
        pltpu.make_async_copy(src, dst, load_sems.at[i])
        for i, (src, dst) in enumerate(
            (
                (q_hbm, q_ref),
                (tree_hbm, tree_ref),
                (pool_hbm.at[pl.ds(0, own)], own_ref),
                (w_hbm, w_ref),
            )
        )
    ]
    for load in loads:
        load.start()

    barrier = pltpu.get_barrier_semaphore()
    for where in ({"req": before}, {"req": after}, {"tp": mate1}, {"tp": mate2}):
        pl.semaphore_signal(barrier, inc=1, device_id=where, device_id_type=MESH)
    pl.semaphore_wait(barrier, 4)

    kn, vn = spill // K_PIECES, spill // V_PIECES
    k_copies = [
        pltpu.make_async_remote_copy(
            src_ref=pool_hbm.at[pl.ds(own + i * kn, kn), :, pl.ds(0, HEAD_SIZE)],
            dst_ref=k_ref.at[pl.ds(i * kn, kn)],
            send_sem=ks_sems.at[i],
            recv_sem=kr_sems.at[i],
            device_id={"req": before},
            device_id_type=MESH,
        )
        for i in range(K_PIECES)
    ]
    v_copies = [
        pltpu.make_async_remote_copy(
            src_ref=pool_hbm.at[pl.ds(own + i * vn, vn), :, pl.ds(HEAD_SIZE, HEAD_SIZE)],
            dst_ref=v_ref.at[pl.ds(i * vn, vn)],
            send_sem=vs_sems.at[i],
            recv_sem=vr_sems.at[i],
            device_id={"req": before},
            device_id_type=MESH,
        )
        for i in range(V_PIECES)
    ]
    for copy in k_copies + v_copies:
        copy.start()

    square = (tokens, tokens)
    sub = lax.broadcasted_iota(jnp.int32, square, 0).astype(f32)
    lane = lax.broadcasted_iota(jnp.int32, square, 1).astype(f32)
    spread_sub = lax.broadcasted_iota(jnp.int32, (tree, tokens), 0)
    spread_lane = lax.broadcasted_iota(jnp.int32, (tree, tokens), 1)
    parents = parents_ref[...].astype(f32)
    parent_row = jnp.zeros((1, tokens), f32)
    for r in range(requests):
        shifted = jnp.where(parents[r : r + 1] < 0, 256.0, parents[r : r + 1] + r * tree)
        spread = (spread_sub + r * tree == spread_lane).astype(f32)
        parent_row += jnp.dot(shifted, spread, preferred_element_type=f32)
    reach_t = ((parent_row == sub) | (sub == lane)).astype(f32)
    for _ in range((tree - 1).bit_length()):
        half = reach_t.astype(bf16)
        reach_t = jnp.minimum(jnp.dot(half, half, preferred_element_type=f32), 1.0)
    reach = reach_t.T
    lane_row = lax.broadcasted_iota(jnp.int32, (1, tokens), 1)
    leaf = jnp.zeros(square, jnp.bool_)
    first_slot = jnp.zeros((1, tokens), f32)
    for r in range(requests):
        leaf = leaf | (sub == (acc_ref[r] + r * tree).astype(f32))
        first_slot = jnp.where(lane_row >= r * tree, float(r * tree), first_slot)
    kept_mask = jnp.sum(jnp.where(leaf, reach, 0.0), axis=0, keepdims=True)
    depth = jnp.sum(reach_t, axis=0, keepdims=True) - 1.0 + first_slot
    selector = jnp.where((depth == sub) & (kept_mask > 0.5), 1.0, 0.0).astype(bf16)
    loads[1].wait()
    kept = jnp.dot(selector, tree_ref[...], preferred_element_type=f32)
    kept_ref[...] = kept.astype(bf16)
    tree_bias = jnp.where(reach > 0.5, 0.0, very_negative)

    loads[0].wait()
    loads[2].wait()
    page_lane = lax.broadcasted_iota(jnp.int32, (1, page), 1)

    def bias_of(visible):
        return jnp.where(page_lane < visible, 0.0, very_negative)

    def query(r):
        return jnp.concatenate(
            [
                q_ref[r * tree : (r + 1) * tree, g * HEAD_SIZE : (g + 1) * HEAD_SIZE]
                for g in range(group)
            ],
            axis=0,
        )

    first = tokens + LOCAL * page
    for r in range(requests):
        q = query(r)
        s = dot_t(q, tree_ref[:, :HEAD_SIZE]).reshape(group, tree, tokens)
        s = s + tree_bias[r * tree : (r + 1) * tree][None]
        s_ref[r, :, 0:tokens] = s.reshape(rows, tokens)
        for k in range(LOCAL):
            keys = own_ref[table_ref[r, k]][:, :HEAD_SIZE]
            at = tokens + k * page
            s_ref[r, :, at : at + page] = dot_t(q, keys) + bias_of(len_ref[r] - k * page)

    for i in range(K_PIECES):
        k_copies[i].wait_recv()
        for r in range(requests):
            keys = k_ref[i * kn : (i + 1) * kn].reshape(kn * page, HEAD_SIZE)
            s = dot_t(query(r), keys)
            for j in range(kn):
                slot = i * kn + j
                visible = jnp.int32(0)
                for k in range(LOCAL, max_pages):
                    here = table_ref[r, k] == own + slot
                    visible = jnp.maximum(
                        visible, jnp.where(here, len_ref[r] - k * page, 0)
                    )
                at = first + slot * page
                s_ref[r, :, at : at + page] = s[:, j * page : (j + 1) * page] + bias_of(visible)

    width = s_ref.shape[2]
    for r in range(requests):

        def weigh(g, _):
            at = pl.ds(pl.multiple_of(g * tree, tree), tree)
            s = s_ref[r, at, :]
            top = jnp.max(s, axis=1, keepdims=True)
            p_ref[r, at, :] = jnp.exp((s - top) * scale).astype(bf16)
            return 0

        lax.fori_loop(0, group, weigh, 0)

    ones = jnp.ones((page, HEAD_SIZE), bf16)

    def with_ones(values):
        return jnp.concatenate([values, ones], axis=1)

    for r in range(requests):
        values = [with_ones(tree_ref[:, HEAD_SIZE:])] + [
            with_ones(own_ref[table_ref[r, k]][:, HEAD_SIZE:]) for k in range(LOCAL)
        ]
        sum_ref[r] = jnp.dot(
            p_ref[r, :, 0:first], jnp.concatenate(values, axis=0), preferred_element_type=f32
        )
    for i in range(V_PIECES):
        v_copies[i].wait_recv()
        values = jnp.concatenate([with_ones(v_ref[i * vn + j]) for j in range(vn)], axis=0)
        at = first + i * vn * page
        for r in range(requests):
            more = jnp.dot(
                p_ref[r, :, at : at + vn * page], values, preferred_element_type=f32
            )
            if i < V_PIECES - 1:
                sum_ref[r] += more
            else:
                total = sum_ref[r] + more
                attention = (total[:, :HEAD_SIZE] / total[:, HEAD_SIZE:]).astype(bf16)
                for g in range(group):
                    att_ref[
                        r * tree : (r + 1) * tree, g * HEAD_SIZE : (g + 1) * HEAD_SIZE
                    ] = attention[g * tree : (g + 1) * tree]

    loads[3].wait()
    out_rows = tokens // tp_size

    def first_copy(j):
        return pltpu.make_async_remote_copy(
            src_ref=send1.at[j, 1 - low],
            dst_ref=recv1.at[j],
            send_sem=s1_sems.at[j],
            recv_sem=r1_sems.at[j],
            device_id={"tp": mate1},
            device_id_type=MESH,
        )

    def second_copy(j):
        return pltpu.make_async_remote_copy(
            src_ref=send2.at[j],
            dst_ref=recv2.at[j],
            send_sem=s2_sems.at[j],
            recv_sem=r2_sems.at[j],
            device_id={"tp": mate2},
            device_id_type=MESH,
        )

    def pass_on(j):
        first_copy(j).wait_recv()
        theirs = part_ref[j, mate2] + recv1[j, 1 - high].astype(f32)
        send2[j] = theirs.astype(bf16)
        second_copy(j).start()

    for j in range(chunks):
        part = jnp.dot(
            att_ref[...], w_ref[:, j * COLS : (j + 1) * COLS], preferred_element_type=f32
        )
        for i in range(tp_size):
            piece = part[i * out_rows : (i + 1) * out_rows]
            part_ref[j, i] = piece
            send1[j, i % 2, i // 2] = piece.astype(bf16)
        first_copy(j).start()
        if j >= 2:
            pass_on(j - 2)
    for j in range(chunks - 2, chunks):
        pass_on(j)
    for j in range(chunks):
        second_copy(j).wait_recv()
        mine = part_ref[j, tp] + recv1[j, high].astype(f32) + recv2[j].astype(f32)
        out_ref[:, j * COLS : (j + 1) * COLS] = mine.astype(bf16)
    for copy in k_copies + v_copies:
        copy.wait_send()
    for j in range(chunks):
        first_copy(j).wait_send()
        second_copy(j).wait_send()


def shards(queries, tree_kv, page_pool, page_table, cache_len, parents, accepted, o_weight):
    requests = page_table.shape[0]
    tree = parents.shape[1]
    tokens, features = queries.shape
    pool, _, page, kv = page_pool.shape
    own = requests * LOCAL
    spill = pool - own
    rows = features // HEAD_SIZE * tree
    width = tokens + (LOCAL + spill) * page
    d_out = o_weight.shape[1]
    tp = lax.axis_size("tp")
    out_rows = tokens // tp
    chunks = d_out // COLS
    smem = pl.BlockSpec(memory_space=pltpu.SMEM)
    vmem = pl.BlockSpec(memory_space=pltpu.VMEM)
    anywhere = pl.BlockSpec(memory_space=pl.ANY)
    dma = pltpu.SemaphoreType.DMA
    projected, kept = pl.pallas_call(
        kernel,
        out_shape=(
            jax.ShapeDtypeStruct((out_rows, d_out), bf16),
            jax.ShapeDtypeStruct((tokens, kv), bf16),
        ),
        in_specs=[smem, smem, smem, vmem, anywhere, anywhere, anywhere, anywhere],
        out_specs=(vmem, vmem),
        scratch_shapes=[
            pltpu.VMEM((tokens, features), bf16),
            pltpu.VMEM((tokens, kv), bf16),
            pltpu.VMEM((own, page, kv), bf16),
            pltpu.VMEM(o_weight.shape, bf16),
            pltpu.VMEM((spill, page, HEAD_SIZE), bf16),
            pltpu.VMEM((spill, page, HEAD_SIZE), bf16),
            pltpu.VMEM((requests, rows, width), f32),
            pltpu.VMEM((requests, rows, width), bf16),
            pltpu.VMEM((requests, rows, 2 * HEAD_SIZE), f32),
            pltpu.VMEM((tokens, features), bf16),
            pltpu.VMEM((chunks, tp, out_rows, COLS), f32),
            pltpu.VMEM((chunks, 2, tp // 2, out_rows, COLS), bf16),
            pltpu.VMEM((chunks, tp // 2, out_rows, COLS), bf16),
            pltpu.VMEM((chunks, out_rows, COLS), bf16),
            pltpu.VMEM((chunks, out_rows, COLS), bf16),
            dma((4,)),
            dma((K_PIECES,)),
            dma((K_PIECES,)),
            dma((V_PIECES,)),
            dma((V_PIECES,)),
            dma((chunks,)),
            dma((chunks,)),
            dma((chunks,)),
            dma((chunks,)),
        ],
        compiler_params=pltpu.CompilerParams(
            collective_id=0, has_side_effects=True, vmem_limit_bytes=40 * 2**20
        ),
    )(
        page_table,
        cache_len,
        accepted,
        parents,
        queries,
        tree_kv.reshape(tokens, kv),
        page_pool.reshape(pool, page, kv),
        o_weight,
    )
    return projected, kept.reshape(tokens, 1, kv)


def solution(mesh):
    in_specs = (
        P("req", "tp"),
        P("req", "tp", None),
        P("req", "tp", None, None),
        P("req", None),
        P("req"),
        P("req", None),
        P("req"),
        P("tp", None),
    )
    out_specs = (P(("req", "tp"), None), P("req", "tp", None))
    return jax.shard_map(shards, mesh=mesh, in_specs=in_specs, out_specs=out_specs, check_vma=False)
```

time: 110 us -> 35 us (0.32); the launches traced: 108 us -> 34.7 us
  Pallas kernels: 0 us -> 25.3 us
  other arithmetic: 25.1 us -> 0 us
  blocking collectives: 23.2 us -> 0 us
  local copies, waits for them, and re-layouts: 31.3 us -> 8.75 us
  matrix products: 14.8 us -> 0 us
  waiting for transfers between devices: 8.62 us -> 0 us
  starting transfers between devices: 4.08 us -> 0 us
    pallas_call x0 -> x1, Pallas kernels: none -> 25.3 us  [shards(): pl.pallas_call(kernel, out_shape=(jax.ShapeDtypeStruct((out_rows, d_out),...]
    psum x1 -> x0, blocking collectives: 23.2 us -> none  [shards(): lax.psum(jnp.dot(attention, o_weight, preferred_element_type=jnp.float32)...]
    dot_general x19 -> x0, matrix products: 14.8 us -> none  [the longest x4 4.11 us: pages_partial(): jnp.einsum('tgd,knd->tgkn', query_rows, pages[..., :head_dim], preferred_...]
    ppermute x5 -> x0, waiting for transfers between devices: 8.62 us -> none  [from_behind(): return lax.ppermute(block, axis, route)]
    gather x4 -> x0, local copies, waits for them, and re-layouts: 8.31 us -> none  [one_request(): pages = jnp.take(pool_slots, table_row, axis=0)]
    unnamed x22 -> x18, local copies, waits for them, and re-layouts: 2.28 us -> 8.75 us
    lt x4 -> x0, other arithmetic: 5.47 us -> none  [one_request(): visible = positions < length]
    dynamic_slice x4 -> x0, local copies, waits for them, and re-layouts: 5.16 us -> none  [sweep_all(): return lax.map(one_request, (query_rows, tables, lengths))]
  transfers between devices with their start and end apart: 5 -> 0, of which waited for: 2 -> 0; matrix products, arithmetic and copies ran while one was open for 32% -> 0% of each run, Pallas kernels for 0% -> 0%
where the time goes in v1:
time: 35 us; the launch traced here: 34.7 us
  Pallas kernels  25.3 us (72%)
  local copies, waits for them, and re-layouts  8.75 us (25%)
  between operations  0.66 us (2%)
    pallas_call x1, Pallas kernels, shards(): pl.pallas_call(kernel, out_shape=(jax.ShapeDtypeStruct((out_rows, d_out),...  25.3 us
    unnamed x18, local copies, waits for them, and re-layouts  8.75 us

profile of v1, /device:TPU:27, one launch (start us, length us, event | category | flops | bytes accessed | tf_op | source)
XLA Modules:
  0.0 34.7 jit_solution(3076901118205776926)
XLA Ops:
  0.6 0.0 copy-start
  0.6 1.9 %copy-done = bf16[896,1792]{1,0:T(8,128)(2,1)S(1)} copy-done((bf16[896,1792]{1,0:T(8,128)(2,1)S(1)}, bf16[896,1792]{1,0:T(8,128)(2,1)}, u32[]{:S(2)}) %copy-start) | copy-done | bytes 3211288
  2.5 0.0 copy-start.1
  2.5 1.1 %copy-done.1 = bf16[12,1,128,256]{3,2,1,0:T(8,128)(2,1)S(1)} copy-done((bf16[12,1,128,256]{3,2,1,0:T(8,128)(2,1)S(1)}, bf16[12,1,128,256]{3,2,1,0:T(8,128)(2,1)}, u32[]{:S(2)}) %copy-start.1) | copy-done | bytes 786456
  3.7 0.0 copy-start.2
  3.7 0.9 %copy-done.2 = bf16[128,896]{1,0:T(8,128)(2,1)S(1)} copy-done((bf16[128,896]{1,0:T(8,128)(2,1)S(1)}, bf16[128,896]{1,0:T(8,128)(2,1)}, u32[]{:S(2)}) %copy-start.2) | copy-done | bytes 229400
  4.6 0.0 copy-start.3
  4.6 0.8 %copy-done.3 = bf16[128,1,256]{2,0,1:T(8,128)(2,1)S(1)} copy-done((bf16[128,1,256]{2,0,1:T(8,128)(2,1)S(1)}, bf16[128,1,256]{2,0,1:T(8,128)(2,1)}, u32[]{:S(2)}) %copy-start.3) | copy-done | bytes 65560
  5.5 0.0 copy-start.4
  5.5 0.7 %copy-done.4 = s32[2,8]{1,0:T(2,128)S(1)} copy-done((s32[2,8]{1,0:T(2,128)S(1)}, s32[2,8]{1,0:T(2,128)}, u32[]{:S(2)}) %copy-start.4) | copy-done | bytes 88
  6.1 0.0 copy-start.5
  6.1 0.7 %copy-done.5 = s32[2,64]{1,0:T(2,128)S(1)} copy-done((s32[2,64]{1,0:T(2,128)S(1)}, s32[2,64]{1,0:T(2,128)}, u32[]{:S(2)}) %copy-start.5) | copy-done | bytes 536
  6.8 0.0 copy-start.6
  6.8 0.7 %copy-done.6 = s32[2]{0:T(128)S(1)} copy-done((s32[2]{0:T(128)S(1)}, s32[2]{0:T(128)}, u32[]{:S(2)}) %copy-start.6) | copy-done | bytes 32
  7.5 0.0 copy-start.7
  7.5 0.7 %copy-done.7 = s32[2]{0:T(128)S(1)} copy-done((s32[2]{0:T(128)S(1)}, s32[2]{0:T(128)}, u32[]{:S(2)}) %copy-start.7) | copy-done | bytes 32
  8.1 25.3 %shard_map.95 = (bf16[32,1792]{1,0:T(8,128)(2,1)S(1)}, bf16[128,256]{1,0:T(8,128)(2,1)S(1)}) custom-call(s32[2,8]{1,0:T(2,128)S(1)} %copy-done.4, s32[2]{0:T(128)S(1)} %copy-done.6, s32[2]{0:T(128)S(1)} %copy-done.7, s32[2,64]{1,0:T(2,128)S(1)} %copy-done.5, bf16[128,896]{1,0:T(8,128)(2,1)S(1)} %copy-done.2, bf16[128,256]{1,0:T(8,128)(2,1)S(1)} %bitcast.4, ...), custom_call_target="tpu_custom_call" | custom-call | tf_op jit(solution)/shard_map/pallas_call | solution.py:313
  33.4 0.6 %copy.12 = bf16[32,1792]{1,0:T(8,128)(2,1)} copy(bf16[32,1792]{1,0:T(8,128)(2,1)S(1)} %get-tuple-element.8) | data formatting | bytes 229376
  34.1 0.6 %copy.13 = bf16[128,1,256]{2,0,1:T(8,128)(2,1)} copy(bf16[128,1,256]{2,0,1:T(8,128)(2,1)S(1)} %bitcast.5) | data formatting | bytes 131072
Async XLA Ops:
  0.6 1.9 %copy-start = (bf16[896,1792]{1,0:T(8,128)(2,1)S(1)}, bf16[896,1792]{1,0:T(8,128)(2,1)}, u32[]{:S(2)}) copy-start(bf16[896,1792]{1,0:T(8,128)(2,1)} %w_hbm.1) | copy-start | bytes 9633796
  2.5 1.1 %copy-start.1 = (bf16[12,1,128,256]{3,2,1,0:T(8,128)(2,1)S(1)}, bf16[12,1,128,256]{3,2,1,0:T(8,128)(2,1)}, u32[]{:S(2)}) copy-start(bf16[12,1,128,256]{3,2,1,0:T(8,128)(2,1)} %param.10) | copy-start | bytes 2359300
  3.7 0.9 %copy-start.2 = (bf16[128,896]{1,0:T(8,128)(2,1)S(1)}, bf16[128,896]{1,0:T(8,128)(2,1)}, u32[]{:S(2)}) copy-start(bf16[128,896]{1,0:T(8,128)(2,1)} %q_hbm.1) | copy-start | bytes 688132
  4.6 0.8 %copy-start.3 = (bf16[128,1,256]{2,0,1:T(8,128)(2,1)S(1)}, bf16[128,1,256]{2,0,1:T(8,128)(2,1)}, u32[]{:S(2)}) copy-start(bf16[128,1,256]{2,0,1:T(8,128)(2,1)} %param.9) | copy-start | bytes 196612
  5.5 0.7 %copy-start.4 = (s32[2,8]{1,0:T(2,128)S(1)}, s32[2,8]{1,0:T(2,128)}, u32[]{:S(2)}) copy-start(s32[2,8]{1,0:T(2,128)} %table_ref.1) | copy-start | bytes 196
  6.1 0.7 %copy-start.5 = (s32[2,64]{1,0:T(2,128)S(1)}, s32[2,64]{1,0:T(2,128)}, u32[]{:S(2)}) copy-start(s32[2,64]{1,0:T(2,128)} %parents_ref.1) | copy-start | bytes 1540
  6.8 0.7 %copy-start.6 = (s32[2]{0:T(128)S(1)}, s32[2]{0:T(128)}, u32[]{:S(2)}) copy-start(s32[2]{0:T(128)} %len_ref.1) | copy-start | bytes 28
  7.5 0.7 %copy-start.7 = (s32[2]{0:T(128)S(1)}, s32[2]{0:T(128)}, u32[]{:S(2)}) copy-start(s32[2]{0:T(128)} %acc_ref.1) | copy-start | bytes 28

commit v2 on v1

--- a/solution.py
+++ b/solution.py
@@ -10,7 +10,7 @@
 
 HEAD_SIZE = 128
 LOCAL = 2
-COLS = 256
+COLS = 896
 K_PIECES = 2
 V_PIECES = 4
 
@@ -313,8 +313,8 @@
     projected, kept = pl.pallas_call(
         kernel,
         out_shape=(
-            jax.ShapeDtypeStruct((out_rows, d_out), bf16),
-            jax.ShapeDtypeStruct((tokens, kv), bf16),
+            pltpu.VMEM((out_rows, d_out), bf16),
+            pltpu.VMEM((tokens, kv), bf16),
         ),
         in_specs=[smem, smem, smem, vmem, anywhere, anywhere, anywhere, anywhere],
         out_specs=(vmem, vmem),
@@ -345,7 +345,7 @@
             dma((chunks,)),
         ],
         compiler_params=pltpu.CompilerParams(
-            collective_id=0, has_side_effects=True, vmem_limit_bytes=40 * 2**20
+            collective_id=0, has_side_effects=True, vmem_limit_bytes=60 * 2**20
         ),
     )(
         page_table,

time: 35 us -> 26.5 us (0.76)
  local copies, waits for them, and re-layouts: 8.75 us -> 1.28 us
  Pallas kernels: 25.3 us -> 24.4 us
    unnamed x18 -> x2, local copies, waits for them, and re-layouts: 8.75 us -> 1.28 us
    pallas_call x1, Pallas kernels: 25.3 us -> 24.4 us  [shards(): pl.pallas_call(kernel, out_shape=(pltpu.VMEM((out_rows, d_out), bf16), pl...]
where the time goes in v2:
time: 26.5 us; the launch traced here: 26.3 us
  Pallas kernels  24.4 us (92%)
  local copies, waits for them, and re-layouts  1.28 us (5%)
  between operations  0.64 us (2%)
    pallas_call x1, Pallas kernels, shards(): pl.pallas_call(kernel, out_shape=(pltpu.VMEM((out_rows, d_out), bf16), pl...  24.4 us
    unnamed x2, local copies, waits for them, and re-layouts  1.28 us

profile of v2, /device:TPU:27, one launch (start us, length us, event | category | flops | bytes accessed | tf_op | source)
XLA Modules:
  0.0 26.3 jit_solution(7904028096023741555)
XLA Ops:
  0.6 24.4 %shard_map.95 = (bf16[32,1792]{1,0:T(8,128)(2,1)S(1)}, bf16[128,256]{1,0:T(8,128)(2,1)S(1)}) custom-call(s32[2,8]{1,0:T(2,128)} %table_ref.1, s32[2]{0:T(128)} %len_ref.1, s32[2]{0:T(128)} %acc_ref.1, s32[2,64]{1,0:T(2,128)} %parents_ref.1, bf16[128,896]{1,0:T(8,128)(2,1)} %q_hbm.1, bf16[128,256]{1,0:T(8,128)(2,1)} %bitcast.5, ...), custom_call_target="tpu_custom_call" | custom-call | tf_op jit(solution)/shard_map/pallas_call | solution.py:313
  25.0 0.6 %copy.12 = bf16[32,1792]{1,0:T(8,128)(2,1)} copy(bf16[32,1792]{1,0:T(8,128)(2,1)S(1)} %get-tuple-element.6) | data formatting | bytes 229376
  25.7 0.6 %copy.13 = bf16[128,1,256]{2,0,1:T(8,128)(2,1)} copy(bf16[128,1,256]{2,0,1:T(8,128)(2,1)S(1)} %bitcast.3) | data formatting | bytes 131072

commit v3 on v2

--- a/solution.py
+++ b/solution.py
@@ -25,16 +25,20 @@
 
 
 def kernel(
-    table_ref,
-    len_ref,
-    acc_ref,
-    parents_ref,
+    table_hbm,
+    len_hbm,
+    acc_hbm,
+    parents_hbm,
     q_hbm,
     tree_hbm,
     pool_hbm,
     w_hbm,
     out_ref,
     kept_ref,
+    table_ref,
+    len_ref,
+    acc_ref,
+    parents_ref,
     q_ref,
     tree_ref,
     own_ref,
@@ -88,11 +92,15 @@
                 (tree_hbm, tree_ref),
                 (pool_hbm.at[pl.ds(0, own)], own_ref),
                 (w_hbm, w_ref),
+                (table_hbm, table_ref),
+                (len_hbm, len_ref),
+                (acc_hbm, acc_ref),
+                (parents_hbm, parents_ref),
             )
         )
     ]
-    for load in loads:
-        load.start()
+    for i in (7, 6, 4, 5, 1, 0, 2, 3):
+        loads[i].start()
 
     barrier = pltpu.get_barrier_semaphore()
     for where in ({"req": before}, {"req": after}, {"tp": mate1}, {"tp": mate2}):
@@ -130,6 +138,8 @@
     lane = lax.broadcasted_iota(jnp.int32, square, 1).astype(f32)
     spread_sub = lax.broadcasted_iota(jnp.int32, (tree, tokens), 0)
     spread_lane = lax.broadcasted_iota(jnp.int32, (tree, tokens), 1)
+    for i in (4, 5, 6, 7):
+        loads[i].wait()
     parents = parents_ref[...].astype(f32)
     parent_row = jnp.zeros((1, tokens), f32)
     for r in range(requests):
@@ -306,7 +316,6 @@
     tp = lax.axis_size("tp")
     out_rows = tokens // tp
     chunks = d_out // COLS
-    smem = pl.BlockSpec(memory_space=pltpu.SMEM)
     vmem = pl.BlockSpec(memory_space=pltpu.VMEM)
     anywhere = pl.BlockSpec(memory_space=pl.ANY)
     dma = pltpu.SemaphoreType.DMA
@@ -316,9 +325,13 @@
             pltpu.VMEM((out_rows, d_out), bf16),
             pltpu.VMEM((tokens, kv), bf16),
         ),
-        in_specs=[smem, smem, smem, vmem, anywhere, anywhere, anywhere, anywhere],
+        in_specs=[anywhere] * 8,
         out_specs=(vmem, vmem),
         scratch_shapes=[
+            pltpu.SMEM(page_table.shape, jnp.int32),
+            pltpu.SMEM(cache_len.shape, jnp.int32),
+            pltpu.SMEM(accepted.shape, jnp.int32),
+            pltpu.VMEM(parents.shape, jnp.int32),
             pltpu.VMEM((tokens, features), bf16),
             pltpu.VMEM((tokens, kv), bf16),
             pltpu.VMEM((own, page, kv), bf16),
@@ -334,7 +347,7 @@
             pltpu.VMEM((chunks, tp // 2, out_rows, COLS), bf16),
             pltpu.VMEM((chunks, out_rows, COLS), bf16),
             pltpu.VMEM((chunks, out_rows, COLS), bf16),
-            dma((4,)),
+            dma((8,)),
             dma((K_PIECES,)),
             dma((K_PIECES,)),
             dma((V_PIECES,)),

time: 26.5 us -> 25.8 us (0.974)
  Pallas kernels: 24.4 us -> 23.7 us
    pallas_call x1, Pallas kernels: 24.4 us -> 23.7 us  [shards(): pl.pallas_call(kernel, out_shape=(pltpu.VMEM((out_rows, d_out), bf16), pl...]
where the time goes in v3:
time: 25.8 us; the launch traced here: 25.6 us
  Pallas kernels  23.7 us (92%)
  local copies, waits for them, and re-layouts  1.28 us (5%)
  between operations  0.64 us (2%)
    pallas_call x1, Pallas kernels, shards(): pl.pallas_call(kernel, out_shape=(pltpu.VMEM((out_rows, d_out), bf16), pl...  23.7 us
    unnamed x2, local copies, waits for them, and re-layouts  1.28 us

profile of v3, /device:TPU:27, one launch (start us, length us, event | category | flops | bytes accessed | tf_op | source)
XLA Modules:
  0.0 25.6 jit_solution(6402784984690311055)
XLA Ops:
  0.6 23.7 %shard_map.95 = (bf16[32,1792]{1,0:T(8,128)(2,1)S(1)}, bf16[128,256]{1,0:T(8,128)(2,1)S(1)}) custom-call(s32[2,8]{1,0:T(2,128)} %table_hbm.1, s32[2]{0:T(128)} %len_hbm.1, s32[2]{0:T(128)} %acc_hbm.1, s32[2,64]{1,0:T(2,128)} %parents_hbm.1, bf16[128,896]{1,0:T(8,128)(2,1)} %q_hbm.1, bf16[128,256]{1,0:T(8,128)(2,1)} %bitcast.5, ...), custom_call_target="tpu_custom_call" | custom-call | tf_op jit(solution)/shard_map/pallas_call | solution.py:322
  24.4 0.6 %copy.12 = bf16[32,1792]{1,0:T(8,128)(2,1)} copy(bf16[32,1792]{1,0:T(8,128)(2,1)S(1)} %get-tuple-element.6) | data formatting | bytes 229376
  25.0 0.6 %copy.13 = bf16[128,1,256]{2,0,1:T(8,128)(2,1)} copy(bf16[128,1,256]{2,0,1:T(8,128)(2,1)S(1)} %bitcast.3) | data formatting | bytes 131072

commit v4 on v3

--- a/solution.py
+++ b/solution.py
@@ -10,7 +10,7 @@
 
 HEAD_SIZE = 128
 LOCAL = 2
-COLS = 896
+FIRST = 384
 K_PIECES = 2
 V_PIECES = 4
 
@@ -18,6 +18,12 @@
 MESH = pl.DeviceIdType.MESH
 f32 = jnp.float32
 bf16 = jnp.bfloat16
+
+
+def column_edges(features):
+    rest = features - FIRST
+    middle = rest // 256 * 128
+    return (0, FIRST, FIRST + middle, features)
 
 
 def dot_t(a, b):
@@ -72,7 +78,9 @@
     own = own_ref.shape[0]
     group = q_ref.shape[1] // HEAD_SIZE
     rows = group * tree
-    chunks = part_ref.shape[0]
+    edges = column_edges(w_ref.shape[1])
+    chunks = len(edges) - 1
+    widths = [b - a for a, b in zip(edges, edges[1:])]
     tp_size = part_ref.shape[1]
     scale = 1.0 / math.sqrt(HEAD_SIZE)
 
@@ -255,8 +263,8 @@
 
     def first_copy(j):
         return pltpu.make_async_remote_copy(
-            src_ref=send1.at[j, 1 - low],
-            dst_ref=recv1.at[j],
+            src_ref=send1.at[j, 1 - low, :, :, pl.ds(0, widths[j])],
+            dst_ref=recv1.at[j, :, :, pl.ds(0, widths[j])],
             send_sem=s1_sems.at[j],
             recv_sem=r1_sems.at[j],
             device_id={"tp": mate1},
@@ -265,8 +273,8 @@
 
     def second_copy(j):
         return pltpu.make_async_remote_copy(
-            src_ref=send2.at[j],
-            dst_ref=recv2.at[j],
+            src_ref=send2.at[j, :, pl.ds(0, widths[j])],
+            dst_ref=recv2.at[j, :, pl.ds(0, widths[j])],
             send_sem=s2_sems.at[j],
             recv_sem=r2_sems.at[j],
             device_id={"tp": mate2},
@@ -275,18 +283,19 @@
 
     def pass_on(j):
         first_copy(j).wait_recv()
-        theirs = part_ref[j, mate2] + recv1[j, 1 - high].astype(f32)
-        send2[j] = theirs.astype(bf16)
+        w = widths[j]
+        theirs = part_ref[j, mate2, :, :w] + recv1[j, 1 - high, :, :w].astype(f32)
+        send2[j, :, :w] = theirs.astype(bf16)
         second_copy(j).start()
 
     for j in range(chunks):
         part = jnp.dot(
-            att_ref[...], w_ref[:, j * COLS : (j + 1) * COLS], preferred_element_type=f32
+            att_ref[...], w_ref[:, edges[j] : edges[j + 1]], preferred_element_type=f32
         )
         for i in range(tp_size):
             piece = part[i * out_rows : (i + 1) * out_rows]
-            part_ref[j, i] = piece
-            send1[j, i % 2, i // 2] = piece.astype(bf16)
+            part_ref[j, i, :, : widths[j]] = piece
+            send1[j, i % 2, i // 2, :, : widths[j]] = piece.astype(bf16)
         first_copy(j).start()
         if j >= 2:
             pass_on(j - 2)
@@ -294,8 +303,10 @@
         pass_on(j)
     for j in range(chunks):
         second_copy(j).wait_recv()
-        mine = part_ref[j, tp] + recv1[j, high].astype(f32) + recv2[j].astype(f32)
-        out_ref[:, j * COLS : (j + 1) * COLS] = mine.astype(bf16)
+        w = widths[j]
+        mine = part_ref[j, tp, :, :w] + recv1[j, high, :, :w].astype(f32)
+        mine = mine + recv2[j, :, :w].astype(f32)
+        out_ref[:, edges[j] : edges[j + 1]] = mine.astype(bf16)
     for copy in k_copies + v_copies:
         copy.wait_send()
     for j in range(chunks):
@@ -315,7 +326,9 @@
     d_out = o_weight.shape[1]
     tp = lax.axis_size("tp")
     out_rows = tokens // tp
-    chunks = d_out // COLS
+    edges = column_edges(d_out)
+    chunks = len(edges) - 1
+    widest = max(b - a for a, b in zip(edges, edges[1:]))
     vmem = pl.BlockSpec(memory_space=pltpu.VMEM)
     anywhere = pl.BlockSpec(memory_space=pl.ANY)
     dma = pltpu.SemaphoreType.DMA
@@ -342,11 +355,11 @@
             pltpu.VMEM((requests, rows, width), bf16),
             pltpu.VMEM((requests, rows, 2 * HEAD_SIZE), f32),
             pltpu.VMEM((tokens, features), bf16),
-            pltpu.VMEM((chunks, tp, out_rows, COLS), f32),
-            pltpu.VMEM((chunks, 2, tp // 2, out_rows, COLS), bf16),
-            pltpu.VMEM((chunks, tp // 2, out_rows, COLS), bf16),
-            pltpu.VMEM((chunks, out_rows, COLS), bf16),
-            pltpu.VMEM((chunks, out_rows, COLS), bf16),
+            pltpu.VMEM((chunks, tp, out_rows, widest), f32),
+            pltpu.VMEM((chunks, 2, tp // 2, out_rows, widest), bf16),
+            pltpu.VMEM((chunks, tp // 2, out_rows, widest), bf16),
+            pltpu.VMEM((chunks, out_rows, widest), bf16),
+            pltpu.VMEM((chunks, out_rows, widest), bf16),
             dma((8,)),
             dma((K_PIECES,)),
             dma((K_PIECES,)),

time: 25.8 us -> 25.8 us (level)
  no operation moved by 1% of the time
where the time goes in v4:
time: 25.8 us; the launch traced here: 25.7 us
  Pallas kernels  23.8 us (92%)
  local copies, waits for them, and re-layouts  1.28 us (5%)
  between operations  0.64 us (2%)
    pallas_call x1, Pallas kernels, shards(): pl.pallas_call(kernel, out_shape=(pltpu.VMEM((out_rows, d_out), bf16), pl...  23.8 us
    unnamed x2, local copies, waits for them, and re-layouts  1.28 us

profile of v4, /device:TPU:27, one launch (start us, length us, event | category | flops | bytes accessed | tf_op | source)
XLA Modules:
  0.0 25.7 jit_solution(15703306559622907387)
XLA Ops:
  0.6 23.8 %shard_map.95 = (bf16[32,1792]{1,0:T(8,128)(2,1)S(1)}, bf16[128,256]{1,0:T(8,128)(2,1)S(1)}) custom-call(s32[2,8]{1,0:T(2,128)} %table_hbm.1, s32[2]{0:T(128)} %len_hbm.1, s32[2]{0:T(128)} %acc_hbm.1, s32[2,64]{1,0:T(2,128)} %parents_hbm.1, bf16[128,896]{1,0:T(8,128)(2,1)} %q_hbm.1, bf16[128,256]{1,0:T(8,128)(2,1)} %bitcast.5, ...), custom_call_target="tpu_custom_call" | custom-call | tf_op jit(solution)/shard_map/pallas_call | solution.py:335
  24.4 0.6 %copy.12 = bf16[32,1792]{1,0:T(8,128)(2,1)} copy(bf16[32,1792]{1,0:T(8,128)(2,1)S(1)} %get-tuple-element.6) | data formatting | bytes 229376
  25.1 0.6 %copy.13 = bf16[128,1,256]{2,0,1:T(8,128)(2,1)} copy(bf16[128,1,256]{2,0,1:T(8,128)(2,1)S(1)} %bitcast.3) | data formatting | bytes 131072
